TPU v7x, 512 devices: a whole 4x8x8 slice. The times are simulated.
512 devices in a mesh: dp: 32 (over y, z_lo), tp: 16 (over z_hi, x, core).
Axes of the slice: x: 4, y: 8, z: 8 (z_hi: 2, z_lo: 4; z = z_hi * 4 + z_lo), core: 2. Of those that a mesh axis runs over, the one named last changes fastest.
Arguments:
- activations: bfloat16 [64, 1024, 3584], P('dp', 'tp'), may hold values from -6 to 6
- out_grads: bfloat16 [64, 1024, 4096], P('dp', None, 'tp'), may hold values from -1.5 to 1.5
- clip_bound: float32 [1], replicated, may hold values from 3584 to 7168
Outputs:
- clipped_sum: float32 [3584, 4096], P('dp', 'tp')
All inputs are finite; a program needn't handle non-finite values.
Results may differ from a plain program's by a relative error of at most 0.0003.
Values may be sent and summed in bfloat16 or wider, within the bound.
A program may use at most 64 MiB of HBM per device.

v0:
```python
import jax
import jax.numpy as jnp
from jax import lax
from jax.sharding import PartitionSpec as P


def clip_weights(square_sums, clip_bound):
    norm_values = jnp.sqrt(square_sums)
    return jnp.minimum(jnp.float32(1.0), clip_bound[0] / (norm_values + 1e-06))


def body(activations, out_grads, clip_bound):
    whole = lax.all_gather(activations, "tp", axis=1, tiled=True)
    per_example = jnp.einsum("etd,etq->edq", whole, out_grads, preferred_element_type=jnp.float32)
    partial_value = jnp.sum(per_example * per_example, axis=(1, 2))
    square_sums = lax.psum(partial_value, "tp")
    factors = clip_weights(square_sums, clip_bound)
    weighted = jnp.einsum("e,edq->dq", factors, per_example, precision=lax.Precision.HIGHEST)
    return lax.psum_scatter(weighted, "dp", scatter_dimension=0, tiled=True)


def solution(mesh):
    return jax.shard_map(
        body,
        mesh=mesh,
        in_specs=(P("dp", "tp", None), P("dp", None, "tp"), P()),
        out_specs=P("dp", "tp"),
        check_vma=False,
    )
```

profile of v0, /device:TPU:6, one launch (start us, length us, event | category | flops | bytes accessed | tf_op | source)
XLA Modules:
  0.0 457.3 jit_solution(14687276970869819420)
XLA Ops:
  6.5 0.0 copy-start
  6.5 0.0 all-gather.2.cloned.1.call-start
  6.5 0.7 all-gather.2.cloned.1.call-update
  7.3 0.0 reduce-scatter.2.cloned.1.call-start
  8.0 169.6 %all-gather.2.cloned.1.call-done = bf16[2,1024,3584]{2,1,0:T(8,128)(2,1)} async-done(((bf16[2,64,3584]{2,1,0:T(8,128)(2,1)}), bf16[2,1024,3584]{2,1,0:T(8,128)(2,1)}) %all-gather.2.cloned.1.call-update) | async-done | bytes 14680080 | tf_op jit(solution)/shard_map/all_gather | solution.py:13
  177.6 0.0 copy-done
  177.6 10.9 %multiply_reduce_fusion = (f32[2]{0:T(128)S(1)}, f32[2,3584,256]{2,1,0:T(8,128)}) fusion(bf16[2,1024,3584]{2,1,0:T(8,128)(2,1)} %all-gather.2.cloned.1.call-done, bf16[2,1024,256]{2,1,0:T(8,128)(2,1)S(1)} %copy-done), kind=kOutput, calls=%fused_computation | convolution fusion | flops 3761766400 | bytes 23068680 | tf_op jit(solution)/shard_map/etd,etq->edq/dot_general | solution.py:14
  188.5 36.5 %psum.7 = f32[2]{0:T(128)S(1)} all-reduce(f32[2]{0:T(128)S(1)} %get-tuple-element.5), channel_id=1, replica_groups=mesh['dp'=32,'tp'=16] {'tp'}, use_global_device_ids=true, to_apply=%region_1.0 | all-reduce | flops 2 | bytes 16 | tf_op jit(solution)/shard_map/psum | solution.py:16
  225.1 47.3 %fusion = f32[1,3584,256]{2,0,1:T(1,128)S(1)} fusion(f32[2,3584,256]{2,1,0:T(8,128)} %get-tuple-element.6, f32[2]{0:T(128)S(1)} %psum.7, f32[]{:T(128)} %bitcast.9), kind=kOutput, calls=%fused_computation.1 | convolution fusion | flops 22020102 | bytes 11010060 | tf_op jit(solution)/shard_map/e,edq->dq/dot_general | solution.py:18
  272.4 2.0 copy.9
  274.4 0.0 reduce-scatter.2.cloned.1.call-update
  274.4 176.1 %reduce-scatter.2.cloned.1.call-done = f32[112,256]{1,0:T(8,128)} async-done(((f32[3584,256]{1,0:T(8,128)}), f32[112,256]{1,0:T(8,128)}) %reduce-scatter.2.cloned.1.call-update) | async-done | bytes 114704 | tf_op jit(solution)/shard_map/reduce_scatter | solution.py:19
Async XLA Ops:
  6.5 171.0 %copy-start = (bf16[2,1024,256]{2,1,0:T(8,128)(2,1)S(1)}, bf16[2,1024,256]{2,1,0:T(8,128)(2,1)}, u32[]{:S(2)}) copy-start(bf16[2,1024,256]{2,1,0:T(8,128)(2,1)} %param.4) | copy-start | bytes 3145732
  6.5 171.0 %all-gather.2.cloned.1.call-start = ((), (), s32[]{:S(2)}) async-start(), calls=%async_computation.1 | async-start | bytes 15597568 | tf_op jit(solution)/shard_map/all_gather | solution.py:13
  7.3 443.3 %reduce-scatter.2.cloned.1.call-start = ((), (), s32[]{:S(2)}) async-start(), calls=%async_computation.2 | async-start | bytes 3784704 | tf_op jit(solution)/shard_map/reduce_scatter | solution.py:19
Sparse Core Ops, SparseCore 0:
  10.7 166.8 all-gather.1
  274.6 175.9 reduce-scatter.1
where the time goes:
time: 458 us; the launch traced here: 457 us
  waiting for transfers between devices  346 us (76%)
  matrix products  58.3 us (13%)
  blocking collectives  36.5 us (8%)
  between operations  14.1 us (3%)
    reduce_scatter x1, waiting for transfers between devices, body(): return lax.psum_scatter(weighted, 'dp', scatter_dimension=0, tiled=True)  176 us
    all_gather x1, waiting for transfers between devices, body(): whole = lax.all_gather(activations, 'tp', axis=1, tiled=True)  170 us
    dot_general x1, matrix products, body(): jnp.einsum('e,edq->dq', factors, per_example, precision=lax.Precision.HIG...  47.3 us
    psum x1, blocking collectives, body(): square_sums = lax.psum(partial_value, 'tp')  36.5 us
    dot_general x1, matrix products, body(): jnp.einsum('etd,etq->edq', whole, out_grads, preferred_element_type=jnp.f...  10.9 us
  transfers between devices with their start and end apart: 2, of which 2 were waited for; matrix products, arithmetic and copies ran while one was open for 0% of the time, Pallas kernels for 0%

commit v1 on v0

v1 whole, which is shorter than its diff:
```python
import math

import jax
import jax.numpy as jnp
from jax import lax
from jax.experimental import pallas as pl
from jax.experimental.pallas import tpu as pltpu
from jax.sharding import PartitionSpec as P

MESH = pl.DeviceIdType.MESH
F32 = jnp.float32
NX, NY, NZL, NZH = 4, 8, 4, 2
HALF = 32
ROWS = 112
TILE = 512
POWER, SHIFT = 11, 120
OFFSET = (0, 1, 3, 2)
OWN, FROM_RIGHT, FROM_LEFT, FAR = 0, 1, 2, 3


def encode(value, bound):
    u = (value.reshape(-1, 8, 256) * (2.0 ** (SHIFT / POWER) / bound)[None]).reshape(value.shape)
    u2 = u * u
    u4 = u2 * u2
    return ((u4 * u4) * (u2 * u)).astype(jnp.bfloat16)


def decode(code, bound):
    code = code.astype(F32)
    size = jnp.exp2(jnp.log(jnp.maximum(jnp.abs(code), 2.0**-126)) * (1.0 / (POWER * math.log(2.0))))
    size = (size.reshape(-1, 8, 256) * (2.0 ** (-SHIFT / POWER) * bound)[None]).reshape(code.shape)
    return jnp.where(code > 0, size, jnp.where(code < 0, -size, 0.0))


def kernel(
    act, grads, clip, out,
    buf, relay, gr, prod, sq, sq_in, top, bound, bound_in, total_out, total_in, sout, sin, yout, yin, zout, zin,
    load_sem, x_s, x_r, f_s, f_r, z_s, z_r, d_s, d_r, n_s, n_r, b_s, b_r, t_s, t_r, s_s, s_r, y_s, y_r, w_s, w_r,
):
    dp, tp = lax.axis_index("dp"), lax.axis_index("tp")
    y, zl = lax.div(dp, 4), lax.rem(dp, 4)
    zh, x, c = lax.div(tp, 8), lax.rem(lax.div(tp, 2), 4), lax.rem(tp, 2)
    z = zh * 4 + zl

    def peer(dx=0, dy=0, dz=0, dc=0):
        nz = lax.rem(z + dz, 8)
        return (
            lax.rem(y + dy, 8) * 4 + lax.rem(nz, 4),
            lax.div(nz, 4) * 8 + lax.rem(x + dx, 4) * 2 + lax.rem(c + dc, 2),
        )

    def line(r):
        return (y * 4 + lax.rem(zl + r, 4), tp)

    tp_peers = [(i, peer(dx=(i // 2) % 4, dz=4 * (i // 8), dc=i % 2)) for i in range(1, 16)]
    z_far = {0: peer(dz=2), 1: peer(dz=6)}
    x_next = {0: peer(dx=1), 1: peer(dx=3)}
    y_next = {0: peer(dy=1), 1: peer(dy=7)}
    other = peer(dc=1)

    def unit(e, far, pos, core, h):
        return buf.at[e, 16 * far + 4 * pos + 2 * core + h]

    def remote(src, dst, s, r, to):
        return pltpu.make_async_remote_copy(
            src_ref=src, dst_ref=dst, send_sem=s, recv_sem=r, device_id=to, device_id_type=MESH
        )

    started = []

    def start(copy):
        copy.start()
        started.append(copy)

    def x_copy(e, far, d, h):
        return remote(
            unit(e, far, OWN, 0, h), unit(e, far, FROM_LEFT if d == 0 else FROM_RIGHT, 0, h),
            x_s.at[e, far, d, h], x_r.at[e, far, d, h], x_next[d],
        )

    def f_copy(e, far, d):
        return remote(
            unit(e, far, FROM_LEFT if d == 0 else FROM_RIGHT, 0, d), unit(e, far, FAR, 0, d),
            f_s.at[e, far, d], f_r.at[e, far, d], x_next[d],
        )

    def z_copy(e, d, leg):
        src = unit(e, 0, OWN, 0, d) if leg == 0 else relay.at[e, d]
        dst = relay.at[e, d] if leg == 0 else unit(e, 1, OWN, 0, d)
        return remote(src, dst, z_s.at[e, d, leg], z_r.at[e, d, leg], z_far[d])

    def d_copy(e, far, pos, h):
        return remote(
            unit(e, far, pos, 0, h), unit(e, far, pos, 1, h),
            d_s.at[e, far, pos, h], d_r.at[e, far, pos, h], other,
        )

    loads = {
        (e, h): pltpu.make_async_copy(
            act.at[e, pl.ds(h * HALF, HALF)], unit(e, 0, OWN, 0, h), load_sem.at[e, h]
        )
        for e in range(2) for h in range(2)
    }
    for load in loads.values():
        load.start()

    barrier = pltpu.get_barrier_semaphore()
    greeted = [to for _, to in tp_peers] + list(z_far.values())
    greeted += [peer(dy=k) for k in range(1, 8)] + [line(r) for r in range(1, 4)]
    for to in greeted:
        pl.semaphore_signal(barrier, inc=1, device_id=to, device_id_type=MESH)
    pl.semaphore_wait(barrier, len(greeted))

    for e in range(2):
        for h in range(2):
            loads[e, h].wait()
        if e == 0:
            start(z_copy(0, 0, 0))
            start(z_copy(0, 1, 0))
        for h in range(2):
            for d in range(2):
                start(x_copy(e, 0, d, h if d == 0 else 1 - h))
        for h in range(2):
            start(d_copy(e, 0, OWN, h))

    for e in range(2):
        for far in range(2):
            for pos in range(4):
                for core in range(2):
                    block = (
                        lax.rem(zh + far, 2) * 8 + lax.rem(x + OFFSET[pos], 4) * 2 + lax.rem(c + core, 2)
                    )
                    rows = pl.ds(pl.multiple_of(block * 64, 64), 64)
                    gr[e, 8 * far + 2 * pos + core] = grads[e, rows, :]

    def pass_relay(e):
        for d in range(2):
            z_copy(e, d, 0).wait_recv()
            start(z_copy(e, d, 1))

    def take_z(e):
        for d in range(2):
            z_copy(e, d, 1).wait_recv()
            for k in range(2):
                start(x_copy(e, 1, k, d))
            start(d_copy(e, 1, OWN, d))

    def take_x(e, far):
        for step in range(2):
            for d in range(2):
                h = d if step == 0 else 1 - d
                x_copy(e, far, d, h).wait_recv()
                if step == 0:
                    start(f_copy(e, far, d))
                start(d_copy(e, far, FROM_LEFT if d == 0 else FROM_RIGHT, h))

    def take_far(e, far):
        for d in range(2):
            f_copy(e, far, d).wait_recv()
            start(d_copy(e, far, FAR, d))

    def wait_core(e, far, positions):
        for pos in positions:
            for h in range(2):
                d_copy(e, far, pos, h).wait_recv()

    def multiply(e, lo, hi):
        first, last = lo == 0, hi == 8
        k = (hi - lo) * 128
        right = gr[e, 2 * lo:2 * hi].reshape(k, 256)

        def body(j, state):
            total, most = state
            cols = pl.ds(pl.multiple_of(j * TILE, TILE), TILE)
            left = buf[e, 4 * lo:4 * hi, :, cols].reshape(k, TILE)
            part = lax.dot_general(left, right, (((0,), (0,)), ((), ())), preferred_element_type=F32)
            if not first:
                part = part + prod[e, cols, :]
            prod[e, cols, :] = part
            if last:
                total = total + jnp.sum((part * part).reshape(TILE // 8, 8, 256), axis=0)
                most = jnp.maximum(most, jnp.max(jnp.abs(part).reshape(TILE // 8, 8, 256), axis=0))
            return total, most

        none = jnp.zeros((8, 256), F32)
        total, most = lax.fori_loop(0, 3584 // TILE, body, (none, none))
        if last:
            sq[e] = total
            top[e] = most
            for i, to in tp_peers:
                start(remote(sq.at[e], sq_in.at[e, i], n_s.at[e, i], n_r.at[e, i], to))

    def begins(d, r):
        return 4 if (r in (1, 3)) == (d == 0) else 3

    def block(e, row_y, r):
        rows = pl.ds(pl.multiple_of((row_y * 4 + lax.rem(zl + r, 4)) * ROWS, 16), ROWS)
        return prod[e, rows, :]

    def ahead(d, dist):
        return lax.rem(y + (dist if d == 0 else 8 - dist), 8)

    def tile_max(value):
        return jnp.broadcast_to(jnp.max(value, axis=(0, 1), keepdims=True), (8, 256))

    order = [(0, 1), (1, 2), (0, 3), (1, 0), (1, 1), (0, 2), (1, 3), (0, 0)]

    def s_copy(e, d, r):
        return remote(sout.at[e, d, r], sin.at[e, d, r], s_s.at[e, d, r], s_r.at[e, d, r], y_next[d])

    def first_hop(e):
        most = tile_max(top[e]) * 1.0001 + 1e-35
        for d, r in order:
            sout[e, d, r] = encode(block(e, ahead(d, begins(d, r)), r), most)
            start(s_copy(e, d, r))
        return most

    def factor(e):
        total = sq[e]
        for i, to in tp_peers:
            remote(sq.at[e], sq_in.at[e, i], n_s.at[e, i], n_r.at[e, i], to).wait_recv()
            total = total + sq_in[e, i]
        norm = jnp.sqrt(jnp.broadcast_to(jnp.sum(total, axis=(0, 1), keepdims=True), (8, 256)))
        return jnp.minimum(1.0, clip[0] / (norm + 1e-06))

    def b_copy(e, k):
        return remote(bound.at[e], bound_in.at[e, k], b_s.at[e, k], b_r.at[e, k], peer(dy=k))

    def send_bound(e, value):
        bound[e] = value
        for k in (1, 7, 2, 6, 3, 5, 4):
            start(b_copy(e, k))

    pass_relay(0)
    take_x(0, 0)
    take_x(1, 0)
    take_z(0)
    start(z_copy(1, 0, 0))
    start(z_copy(1, 1, 0))
    for e in range(2):
        wait_core(e, 0, [OWN, FROM_RIGHT, FROM_LEFT])
        multiply(e, 0, 3)
    pass_relay(1)
    take_far(0, 0)
    take_far(1, 0)
    take_x(0, 1)
    take_z(1)
    wait_core(0, 0, [FAR])
    wait_core(0, 1, [OWN, FROM_RIGHT, FROM_LEFT])
    multiply(0, 3, 7)
    wait_core(1, 0, [FAR])
    wait_core(1, 1, [OWN])
    multiply(1, 3, 5)
    take_far(0, 1)
    wait_core(0, 1, [FAR])
    multiply(0, 7, 8)
    most0 = first_hop(0)
    take_x(1, 1)
    wait_core(1, 1, [FROM_RIGHT, FROM_LEFT])
    multiply(1, 5, 7)
    factor0 = factor(0)
    bound0 = factor0 * most0
    send_bound(0, bound0)
    take_far(1, 1)
    wait_core(1, 1, [FAR])
    multiply(1, 7, 8)
    most1 = first_hop(1)
    factor1 = factor(1)
    bound1 = factor1 * most1
    send_bound(1, bound1)
    mine = bound0 + bound1

    def own(row_y, r):
        terms = [
            scale[None] * block(e, row_y, r).reshape(ROWS // 8, 8, 256)
            for e, scale in enumerate((factor0, factor1))
        ]
        return (terms[0] + terms[1]).reshape(ROWS, 256)

    def t_copy(r):
        return remote(total_out, total_in.at[r], t_s.at[r], t_r.at[r], line(r))

    def y_copy(d, dist, r):
        return remote(
            yout.at[d, dist - 1, r], yin.at[d, dist - 1, r],
            y_s.at[d, dist - 1, r], y_r.at[d, dist - 1, r], y_next[d],
        )

    sums = {}

    def take_bound(d, n):
        k = n if d == 0 else 8 - n
        if not (d == 1 and n == 4):
            for e in range(2):
                b_copy(e, k).wait_recv()
        near = bound_in[0, k] + bound_in[1, k]
        sums[d, n] = near if n == 1 else sums[d, n - 1] + near

    def arrived(d, dist, r):
        steps = begins(d, r) - dist
        if steps > 1:
            y_copy(d, dist + 1, r).wait_recv()
            return decode(yin[d, dist, r], sums[d, steps])
        value = 0.0
        for e in range(2):
            s_copy(e, d, r).wait_recv()
            value = value + decode(sin[e, d, r], bound_in[e, 1 if d == 0 else 7])
        return value

    for steps in (1, 2, 3):
        for d in range(2):
            if (d, steps) not in sums:
                take_bound(d, steps)
        for d, r in order:
            dist = begins(d, r) - steps
            if dist > 0:
                value = own(ahead(d, dist), r) + arrived(d, dist, r)
                yout[d, dist - 1, r] = encode(value, mine + sums[d, steps])
                start(y_copy(d, dist, r))
        if steps == 2:
            for n in (3, 4):
                for d in range(2):
                    if (d, n) not in sums:
                        take_bound(d, n)
            total_out[...] = mine + sums[0, 4] + sums[1, 3]
            for r in range(1, 4):
                start(t_copy(r))

    def w_copy(r):
        return remote(zout.at[r], zin.at[r], w_s.at[r], w_r.at[r], line(r))

    result = None
    for r in (1, 2, 3, 0):
        value = own(y, r)
        for d in range(2):
            value = value + arrived(d, 0, r)
        if r == 0:
            result = value
        else:
            zout[r] = encode(value, total_out[...])
            start(w_copy(r))
    for r in range(1, 4):
        t_copy(r).wait_recv()
        w_copy(r).wait_recv()
        result = result + decode(zin[r], total_in[r])
    out[...] = result
    for copy in started:
        copy.wait_send()


def body(activations, out_grads, clip_bound):
    vmem, dma = pltpu.VMEM, pltpu.SemaphoreType.DMA
    return pl.pallas_call(
        kernel,
        out_shape=jax.ShapeDtypeStruct((ROWS, 256), F32),
        in_specs=[
            pl.BlockSpec(memory_space=pl.ANY),
            pl.BlockSpec(memory_space=pltpu.VMEM),
            pl.BlockSpec(memory_space=pltpu.SMEM),
        ],
        out_specs=pl.BlockSpec(memory_space=pltpu.VMEM),
        scratch_shapes=[
            vmem((2, 32, HALF, 3584), jnp.bfloat16),
            vmem((2, 2, HALF, 3584), jnp.bfloat16),
            vmem((2, 16, 64, 256), jnp.bfloat16),
            vmem((2, 3584, 256), F32),
            vmem((2, 8, 256), F32),
            vmem((2, 16, 8, 256), F32),
            vmem((2, 8, 256), F32),
            vmem((2, 8, 256), F32),
            vmem((2, 8, 8, 256), F32),
            vmem((8, 256), F32),
            vmem((4, 8, 256), F32),
            vmem((2, 2, 4, ROWS, 256), jnp.bfloat16),
            vmem((2, 2, 4, ROWS, 256), jnp.bfloat16),
            vmem((2, 3, 4, ROWS, 256), jnp.bfloat16),
            vmem((2, 3, 4, ROWS, 256), jnp.bfloat16),
            vmem((4, ROWS, 256), jnp.bfloat16),
            vmem((4, ROWS, 256), jnp.bfloat16),
            dma((2, 2)),
            dma((2, 2, 2, 2)), dma((2, 2, 2, 2)),
            dma((2, 2, 2)), dma((2, 2, 2)),
            dma((2, 2, 2)), dma((2, 2, 2)),
            dma((2, 2, 4, 2)), dma((2, 2, 4, 2)),
            dma((2, 16)), dma((2, 16)),
            dma((2, 8)), dma((2, 8)),
            dma((4,)), dma((4,)),
            dma((2, 2, 4)), dma((2, 2, 4)),
            dma((2, 3, 4)), dma((2, 3, 4)),
            dma((4,)), dma((4,)),
        ],
        compiler_params=pltpu.CompilerParams(
            collective_id=0, has_side_effects=True, vmem_limit_bytes=56 * 2**20
        ),
        cost_estimate=pl.CostEstimate(flops=3758096384, bytes_accessed=20000000, transcendentals=1000000),
    )(activations, out_grads, clip_bound)


def solution(mesh):
    return jax.shard_map(
        body,
        mesh=mesh,
        in_specs=(P("dp", "tp", None), P("dp", None, "tp"), P()),
        out_specs=P("dp", "tp"),
        check_vma=False,
    )
```

time: 458 us -> 121 us (0.26)
  waiting for transfers between devices: 346 us -> 0 us
  Pallas kernels: 0 us -> 119 us
  matrix products: 58.3 us -> 0 us
  blocking collectives: 36.5 us -> 0 us
  between operations: 14.1 us -> 0.66 us
    reduce_scatter x1 -> x0, waiting for transfers between devices: 176 us -> none  [body(): return lax.psum_scatter(weighted, 'dp', scatter_dimension=0, tiled=True)]
    all_gather x1 -> x0, waiting for transfers between devices: 170 us -> none  [body(): whole = lax.all_gather(activations, 'tp', axis=1, tiled=True)]
    pallas_call x0 -> x1, Pallas kernels: none -> 119 us  [body(): pl.pallas_call(kernel, out_shape=jax.ShapeDtypeStruct((ROWS, 256), F32),...]
    dot_general x2 -> x0, matrix products: 58.3 us -> none  [the longest x1 47.3 us: body(): jnp.einsum('e,edq->dq', factors, per_example, precision=lax.Precision.HIG...]
    psum x1 -> x0, blocking collectives: 36.5 us -> none  [body(): square_sums = lax.psum(partial_value, 'tp')]
  transfers between devices with their start and end apart: 2 -> 0, of which waited for: 2 -> 0; matrix products, arithmetic and copies ran while one was open for 0% -> 0% of each run, Pallas kernels for 0% -> 0%
where the time goes in v1:
time: 121 us
  Pallas kernels  119 us (98%)
  local copies, waits for them, and re-layouts  1.55 us (1%)
    pallas_call x1, Pallas kernels, body(): pl.pallas_call(kernel, out_shape=jax.ShapeDtypeStruct((ROWS, 256), F32),...  119 us

profile of v1, /device:TPU:6, one launch (start us, length us, event | category | flops | bytes accessed | tf_op | source)
XLA Modules:
  0.0 121.0 jit_solution(17960098813188554135)
XLA Ops:
  0.7 118.8 %shard_map.37 = f32[112,256]{1,0:T(8,128)} custom-call(bf16[2,64,3584]{2,1,0:T(8,128)(2,1)} %act.1, bf16[2,1024,256]{2,1,0:T(8,128)(2,1)} %grads.1, f32[1]{0:T(128)S(6)} %copy.5.clip), custom_call_target="tpu_custom_call" | custom-call | flops 3758096384 | bytes 20000000 | tf_op jit(solution)/shard_map/pallas_call | solution.py:353
  119.5 1.6 %copy.6 = f32[112,256]{1,0:T(8,128)} copy(f32[112,256]{1,0:T(8,128)} %shard_map.37) | data formatting | bytes 229376

commit v2 on v1

--- a/solution.py
+++ b/solution.py
@@ -33,9 +33,9 @@
 
 
 def kernel(
-    act, grads, clip, out,
-    buf, relay, gr, prod, sq, sq_in, top, bound, bound_in, total_out, total_in, sout, sin, yout, yin, zout, zin,
-    load_sem, x_s, x_r, f_s, f_r, z_s, z_r, d_s, d_r, n_s, n_r, b_s, b_r, t_s, t_r, s_s, s_r, y_s, y_r, w_s, w_r,
+    act, grads_in, clip, out,
+    grads, buf, relay, gr, prod, sq, sq_in, top, bound, bound_in, total_out, total_in, sout, sin, yout, yin, zout, zin,
+    load_sem, grads_sem, x_s, x_r, f_s, f_r, z_s, z_r, d_s, d_r, n_s, n_r, b_s, b_r, t_s, t_r, s_s, s_r, y_s, y_r, w_s, w_r,
 ):
     dp, tp = lax.axis_index("dp"), lax.axis_index("tp")
     y, zl = lax.div(dp, 4), lax.rem(dp, 4)
@@ -68,6 +68,11 @@
 
     started = []
 
+    def settle(count):
+        for copy in started[:count]:
+            copy.wait_send()
+        del started[:count]
+
     def start(copy):
         copy.start()
         started.append(copy)
@@ -103,6 +108,8 @@
     }
     for load in loads.values():
         load.start()
+    grads_load = pltpu.make_async_copy(grads_in, grads, grads_sem)
+    grads_load.start()
 
     barrier = pltpu.get_barrier_semaphore()
     greeted = [to for _, to in tp_peers] + list(z_far.values())
@@ -123,6 +130,7 @@
         for h in range(2):
             start(d_copy(e, 0, OWN, h))
 
+    grads_load.wait()
     for e in range(2):
         for far in range(2):
             for pos in range(4):
@@ -248,23 +256,23 @@
     wait_core(0, 0, [FAR])
     wait_core(0, 1, [OWN, FROM_RIGHT, FROM_LEFT])
     multiply(0, 3, 7)
-    wait_core(1, 0, [FAR])
-    wait_core(1, 1, [OWN])
-    multiply(1, 3, 5)
     take_far(0, 1)
     wait_core(0, 1, [FAR])
     multiply(0, 7, 8)
+    take_x(1, 1)
     most0 = first_hop(0)
-    take_x(1, 1)
-    wait_core(1, 1, [FROM_RIGHT, FROM_LEFT])
-    multiply(1, 5, 7)
+    wait_core(1, 0, [FAR])
+    wait_core(1, 1, [OWN, FROM_RIGHT, FROM_LEFT])
+    multiply(1, 3, 7)
     factor0 = factor(0)
     bound0 = factor0 * most0
     send_bound(0, bound0)
     take_far(1, 1)
+    gathered = len(started)
     wait_core(1, 1, [FAR])
     multiply(1, 7, 8)
     most1 = first_hop(1)
+    settle(gathered)
     factor1 = factor(1)
     bound1 = factor1 * most1
     send_bound(1, bound1)
@@ -307,45 +315,49 @@
             value = value + decode(sin[e, d, r], bound_in[e, 1 if d == 0 else 7])
         return value
 
-    for steps in (1, 2, 3):
+    def w_copy(r):
+        return remote(zout.at[r], zin.at[r], w_s.at[r], w_r.at[r], line(r))
+
+    def pass_on(steps, rows):
         for d in range(2):
             if (d, steps) not in sums:
                 take_bound(d, steps)
         for d, r in order:
             dist = begins(d, r) - steps
-            if dist > 0:
+            if r in rows and dist > 0:
                 value = own(ahead(d, dist), r) + arrived(d, dist, r)
                 yout[d, dist - 1, r] = encode(value, mine + sums[d, steps])
                 start(y_copy(d, dist, r))
-        if steps == 2:
-            for n in (3, 4):
-                for d in range(2):
-                    if (d, n) not in sums:
-                        take_bound(d, n)
-            total_out[...] = mine + sums[0, 4] + sums[1, 3]
-            for r in range(1, 4):
-                start(t_copy(r))
-
-    def w_copy(r):
-        return remote(zout.at[r], zin.at[r], w_s.at[r], w_r.at[r], line(r))
-
-    result = None
-    for r in (1, 2, 3, 0):
+
+    def reduced(r):
         value = own(y, r)
         for d in range(2):
             value = value + arrived(d, 0, r)
-        if r == 0:
-            result = value
-        else:
-            zout[r] = encode(value, total_out[...])
-            start(w_copy(r))
-    for r in range(1, 4):
+        return value
+
+    others = (1, 2, 3)
+    pass_on(1, others)
+    pass_on(1, (0,))
+    pass_on(2, others)
+    for n in (3, 4):
+        for d in range(2):
+            take_bound(d, n)
+    total_out[...] = mine + sums[0, 4] + sums[1, 3]
+    for r in others:
+        start(t_copy(r))
+    pass_on(3, others)
+    pass_on(2, (0,))
+    for r in others:
+        zout[r] = encode(reduced(r), total_out[...])
+        start(w_copy(r))
+    pass_on(3, (0,))
+    result = reduced(0)
+    for r in others:
         t_copy(r).wait_recv()
         w_copy(r).wait_recv()
         result = result + decode(zin[r], total_in[r])
     out[...] = result
-    for copy in started:
-        copy.wait_send()
+    settle(len(started))
 
 
 def body(activations, out_grads, clip_bound):
@@ -355,11 +367,12 @@
         out_shape=jax.ShapeDtypeStruct((ROWS, 256), F32),
         in_specs=[
             pl.BlockSpec(memory_space=pl.ANY),
-            pl.BlockSpec(memory_space=pltpu.VMEM),
+            pl.BlockSpec(memory_space=pl.ANY),
             pl.BlockSpec(memory_space=pltpu.SMEM),
         ],
         out_specs=pl.BlockSpec(memory_space=pltpu.VMEM),
         scratch_shapes=[
+            vmem((2, 1024, 256), jnp.bfloat16),
             vmem((2, 32, HALF, 3584), jnp.bfloat16),
             vmem((2, 2, HALF, 3584), jnp.bfloat16),
             vmem((2, 16, 64, 256), jnp.bfloat16),
@@ -378,6 +391,7 @@
             vmem((4, ROWS, 256), jnp.bfloat16),
             vmem((4, ROWS, 256), jnp.bfloat16),
             dma((2, 2)),
+            dma,
             dma((2, 2, 2, 2)), dma((2, 2, 2, 2)),
             dma((2, 2, 2)), dma((2, 2, 2)),
             dma((2, 2, 2)), dma((2, 2, 2)),

time: 121 us -> 119 us (0.983)
  Pallas kernels: 119 us -> 116 us
    pallas_call x1, Pallas kernels: 119 us -> 116 us  [body(): pl.pallas_call(kernel, out_shape=jax.ShapeDtypeStruct((ROWS, 256), F32),...]
where the time goes in v2:
time: 119 us; the launch traced here: 118 us
  Pallas kernels  116 us (97%)
  local copies, waits for them, and re-layouts  1.55 us (1%)
    pallas_call x1, Pallas kernels, body(): pl.pallas_call(kernel, out_shape=jax.ShapeDtypeStruct((ROWS, 256), F32),...  116 us

profile of v2, /device:TPU:6, one launch (start us, length us, event | category | flops | bytes accessed | tf_op | source)
XLA Modules:
  0.0 118.0 jit_solution(15031822313187691487)
XLA Ops:
  0.7 115.8 %shard_map.37 = f32[112,256]{1,0:T(8,128)} custom-call(bf16[2,64,3584]{2,1,0:T(8,128)(2,1)} %act.1, bf16[2,1024,256]{2,1,0:T(8,128)(2,1)} %grads_in.1, f32[1]{0:T(128)S(6)} %copy.5.clip), custom_call_target="tpu_custom_call" | custom-call | flops 3758096384 | bytes 20000000 | tf_op jit(solution)/shard_map/pallas_call | solution.py:365
  116.4 1.6 %copy.6 = f32[112,256]{1,0:T(8,128)} copy(f32[112,256]{1,0:T(8,128)} %shard_map.37) | data formatting | bytes 229376

commit v3 on v2

--- a/solution.py
+++ b/solution.py
@@ -29,7 +29,7 @@
     code = code.astype(F32)
     size = jnp.exp2(jnp.log(jnp.maximum(jnp.abs(code), 2.0**-126)) * (1.0 / (POWER * math.log(2.0))))
     size = (size.reshape(-1, 8, 256) * (2.0 ** (-SHIFT / POWER) * bound)[None]).reshape(code.shape)
-    return jnp.where(code > 0, size, jnp.where(code < 0, -size, 0.0))
+    return jnp.where(code < 0, -size, size)
 
 
 def kernel(
@@ -52,7 +52,7 @@
     def line(r):
         return (y * 4 + lax.rem(zl + r, 4), tp)
 
-    tp_peers = [(i, peer(dx=(i // 2) % 4, dz=4 * (i // 8), dc=i % 2)) for i in range(1, 16)]
+    tp_peers = [(i, peer(dx=(i // 2) % 4, dz=4 * (i // 8), dc=i % 2)) for i in range(15, 0, -1)]
     z_far = {0: peer(dz=2), 1: peer(dz=6)}
     x_next = {0: peer(dx=1), 1: peer(dx=3)}
     y_next = {0: peer(dy=1), 1: peer(dy=7)}
@@ -211,7 +211,7 @@
     def tile_max(value):
         return jnp.broadcast_to(jnp.max(value, axis=(0, 1), keepdims=True), (8, 256))
 
-    order = [(0, 1), (1, 2), (0, 3), (1, 0), (1, 1), (0, 2), (1, 3), (0, 0)]
+    order = [(0, 1), (1, 2), (0, 3), (0, 2), (1, 0), (0, 0), (1, 3), (1, 1)]
 
     def s_copy(e, d, r):
         return remote(sout.at[e, d, r], sin.at[e, d, r], s_s.at[e, d, r], s_r.at[e, d, r], y_next[d])
@@ -245,10 +245,11 @@
     take_z(0)
     start(z_copy(1, 0, 0))
     start(z_copy(1, 1, 0))
-    for e in range(2):
-        wait_core(e, 0, [OWN, FROM_RIGHT, FROM_LEFT])
-        multiply(e, 0, 3)
+    wait_core(0, 0, [OWN, FROM_RIGHT, FROM_LEFT])
+    multiply(0, 0, 3)
     pass_relay(1)
+    wait_core(1, 0, [OWN, FROM_RIGHT, FROM_LEFT])
+    multiply(1, 0, 3)
     take_far(0, 0)
     take_far(1, 0)
     take_x(0, 1)
@@ -259,20 +260,20 @@
     take_far(0, 1)
     wait_core(0, 1, [FAR])
     multiply(0, 7, 8)
+    wait_core(1, 0, [FAR])
+    wait_core(1, 1, [OWN])
+    multiply(1, 3, 5)
     take_x(1, 1)
     most0 = first_hop(0)
-    wait_core(1, 0, [FAR])
-    wait_core(1, 1, [OWN, FROM_RIGHT, FROM_LEFT])
-    multiply(1, 3, 7)
+    wait_core(1, 1, [FROM_RIGHT, FROM_LEFT])
+    multiply(1, 5, 7)
     factor0 = factor(0)
     bound0 = factor0 * most0
     send_bound(0, bound0)
     take_far(1, 1)
-    gathered = len(started)
     wait_core(1, 1, [FAR])
     multiply(1, 7, 8)
     most1 = first_hop(1)
-    settle(gathered)
     factor1 = factor(1)
     bound1 = factor1 * most1
     send_bound(1, bound1)
@@ -294,21 +295,26 @@
             y_s.at[d, dist - 1, r], y_r.at[d, dist - 1, r], y_next[d],
         )
 
-    sums = {}
-
-    def take_bound(d, n):
-        k = n if d == 0 else 8 - n
-        if not (d == 1 and n == 4):
+    bounds, sums = {}, {}
+
+    def near(k):
+        if k not in bounds:
             for e in range(2):
                 b_copy(e, k).wait_recv()
-        near = bound_in[0, k] + bound_in[1, k]
-        sums[d, n] = near if n == 1 else sums[d, n - 1] + near
+            bounds[k] = bound_in[0, k] + bound_in[1, k]
+        return bounds[k]
+
+    def near_sum(d, n):
+        if (d, n) not in sums:
+            value = near(n if d == 0 else 8 - n)
+            sums[d, n] = value if n == 1 else near_sum(d, n - 1) + value
+        return sums[d, n]
 
     def arrived(d, dist, r):
         steps = begins(d, r) - dist
         if steps > 1:
             y_copy(d, dist + 1, r).wait_recv()
-            return decode(yin[d, dist, r], sums[d, steps])
+            return decode(yin[d, dist, r], near_sum(d, steps))
         value = 0.0
         for e in range(2):
             s_copy(e, d, r).wait_recv()
@@ -318,16 +324,12 @@
     def w_copy(r):
         return remote(zout.at[r], zin.at[r], w_s.at[r], w_r.at[r], line(r))
 
-    def pass_on(steps, rows):
-        for d in range(2):
-            if (d, steps) not in sums:
-                take_bound(d, steps)
-        for d, r in order:
-            dist = begins(d, r) - steps
-            if r in rows and dist > 0:
-                value = own(ahead(d, dist), r) + arrived(d, dist, r)
-                yout[d, dist - 1, r] = encode(value, mine + sums[d, steps])
-                start(y_copy(d, dist, r))
+    def pass_on(steps, d, r):
+        dist = begins(d, r) - steps
+        limit = mine + near_sum(d, steps)
+        value = own(ahead(d, dist), r) + arrived(d, dist, r)
+        yout[d, dist - 1, r] = encode(value, limit)
+        start(y_copy(d, dist, r))
 
     def reduced(r):
         value = own(y, r)
@@ -335,24 +337,26 @@
             value = value + arrived(d, 0, r)
         return value
 
-    others = (1, 2, 3)
-    pass_on(1, others)
-    pass_on(1, (0,))
-    pass_on(2, others)
-    for n in (3, 4):
-        for d in range(2):
-            take_bound(d, n)
-    total_out[...] = mine + sums[0, 4] + sums[1, 3]
-    for r in others:
-        start(t_copy(r))
-    pass_on(3, others)
-    pass_on(2, (0,))
-    for r in others:
+    def send_reduced(r):
         zout[r] = encode(reduced(r), total_out[...])
         start(w_copy(r))
-    pass_on(3, (0,))
+
+    for steps, d, r in ((1, 0, 1), (1, 1, 2), (1, 0, 3), (1, 1, 1), (2, 0, 1), (2, 1, 2), (1, 0, 2), (1, 1, 3)):
+        pass_on(steps, d, r)
+    total_out[...] = mine + near_sum(0, 4) + near_sum(1, 3)
+    for r in range(1, 4):
+        start(t_copy(r))
+    for steps, d, r in ((2, 0, 3), (2, 1, 1), (3, 0, 1), (1, 1, 0), (2, 0, 2), (3, 1, 2), (1, 0, 0), (2, 1, 3), (3, 0, 3)):
+        pass_on(steps, d, r)
+    send_reduced(1)
+    pass_on(2, 1, 0)
+    send_reduced(2)
+    pass_on(2, 0, 0)
+    send_reduced(3)
+    pass_on(3, 1, 0)
     result = reduced(0)
-    for r in others:
+    settle(len(started) - 10)
+    for r in range(1, 4):
         t_copy(r).wait_recv()
         w_copy(r).wait_recv()
         result = result + decode(zin[r], total_in[r])

time: 119 us -> 120 us (level)
  no operation moved by 1% of the time
where the time goes in v3:
time: 120 us; the launch traced here: 119 us
  Pallas kernels  116 us (97%)
  local copies, waits for them, and re-layouts  1.55 us (1%)
    pallas_call x1, Pallas kernels, body(): pl.pallas_call(kernel, out_shape=jax.ShapeDtypeStruct((ROWS, 256), F32),...  116 us

profile of v3, /device:TPU:6, one launch (start us, length us, event | category | flops | bytes accessed | tf_op | source)
XLA Modules:
  0.0 118.6 jit_solution(8794334904815595782)
XLA Ops:
  0.7 116.4 %shard_map.37 = f32[112,256]{1,0:T(8,128)} custom-call(bf16[2,64,3584]{2,1,0:T(8,128)(2,1)} %act.1, bf16[2,1024,256]{2,1,0:T(8,128)(2,1)} %grads_in.1, f32[1]{0:T(128)S(6)} %copy.5.clip), custom_call_target="tpu_custom_call" | custom-call | flops 3758096384 | bytes 20000000 | tf_op jit(solution)/shard_map/pallas_call | solution.py:369
  117.1 1.6 %copy.6 = f32[112,256]{1,0:T(8,128)} copy(f32[112,256]{1,0:T(8,128)} %shard_map.37) | data formatting | bytes 229376

commit v4 on v3

--- a/solution.py
+++ b/solution.py
@@ -34,8 +34,8 @@
 
 def kernel(
     act, grads_in, clip, out,
-    grads, buf, relay, gr, prod, sq, sq_in, top, bound, bound_in, total_out, total_in, sout, sin, yout, yin, zout, zin,
-    load_sem, grads_sem, x_s, x_r, f_s, f_r, z_s, z_r, d_s, d_r, n_s, n_r, b_s, b_r, t_s, t_r, s_s, s_r, y_s, y_r, w_s, w_r,
+    grads, buf, relay, gr, prod, sq, sq_in, top, bound, bound_in, line_bound, limit_out, limit_in, sout, sin, yout, yin, zout, zin,
+    load_sem, grads_sem, x_s, x_r, f_s, f_r, z_s, z_r, d_s, d_r, n_s, n_r, b_s, b_r, v_s, v_r, t_s, t_r, s_s, s_r, y_s, y_r, w_s, w_r,
 ):
     dp, tp = lax.axis_index("dp"), lax.axis_index("tp")
     y, zl = lax.div(dp, 4), lax.rem(dp, 4)
@@ -49,8 +49,8 @@
             lax.div(nz, 4) * 8 + lax.rem(x + dx, 4) * 2 + lax.rem(c + dc, 2),
         )
 
-    def line(r):
-        return (y * 4 + lax.rem(zl + r, 4), tp)
+    def line(r, dy=0):
+        return (lax.rem(y + dy, 8) * 4 + lax.rem(zl + r, 4), tp)
 
     tp_peers = [(i, peer(dx=(i // 2) % 4, dz=4 * (i // 8), dc=i % 2)) for i in range(15, 0, -1)]
     z_far = {0: peer(dz=2), 1: peer(dz=6)}
@@ -113,7 +113,8 @@
 
     barrier = pltpu.get_barrier_semaphore()
     greeted = [to for _, to in tp_peers] + list(z_far.values())
-    greeted += [peer(dy=k) for k in range(1, 8)] + [line(r) for r in range(1, 4)]
+    greeted += [peer(dy=k) for k in range(1, 8)]
+    greeted += [line(r, dy) for r in range(1, 4) for dy in (0, 1, 7)]
     for to in greeted:
         pl.semaphore_signal(barrier, inc=1, device_id=to, device_id_type=MESH)
     pl.semaphore_wait(barrier, len(greeted))
@@ -211,16 +212,22 @@
     def tile_max(value):
         return jnp.broadcast_to(jnp.max(value, axis=(0, 1), keepdims=True), (8, 256))
 
-    order = [(0, 1), (1, 2), (0, 3), (0, 2), (1, 0), (0, 0), (1, 3), (1, 1)]
+    order = [(0, 1), (1, 2), (0, 3), (1, 0), (1, 1), (0, 2), (1, 3), (0, 0)]
 
     def s_copy(e, d, r):
         return remote(sout.at[e, d, r], sin.at[e, d, r], s_s.at[e, d, r], s_r.at[e, d, r], y_next[d])
+
+    def w_copy(e, r):
+        return remote(zout.at[e, r], zin.at[e, r], w_s.at[e, r], w_r.at[e, r], line(r))
 
     def first_hop(e):
         most = tile_max(top[e]) * 1.0001 + 1e-35
         for d, r in order:
             sout[e, d, r] = encode(block(e, ahead(d, begins(d, r)), r), most)
             start(s_copy(e, d, r))
+        for r in range(1, 4):
+            zout[e, r] = encode(block(e, y, r), most)
+            start(w_copy(e, r))
         return most
 
     def factor(e):
@@ -286,13 +293,23 @@
         ]
         return (terms[0] + terms[1]).reshape(ROWS, 256)
 
-    def t_copy(r):
-        return remote(total_out, total_in.at[r], t_s.at[r], t_r.at[r], line(r))
+    def v_copy(r):
+        return remote(bound, line_bound.at[r], v_s.at[r], v_r.at[r], line(r))
+
+    for r in range(1, 4):
+        start(v_copy(r))
+
+    def t_copy(d, r):
+        return remote(
+            limit_out.at[d, begins(d, r) - 3], limit_in.at[d, r], t_s.at[d, r], t_r.at[d, r],
+            line(r, 1 if d == 0 else 7),
+        )
 
     def y_copy(d, dist, r):
         return remote(
             yout.at[d, dist - 1, r], yin.at[d, dist - 1, r],
-            y_s.at[d, dist - 1, r], y_r.at[d, dist - 1, r], y_next[d],
+            y_s.at[d, dist - 1, r], y_r.at[d, dist - 1, r],
+            y_next[d] if dist > 1 else line(r, 1 if d == 0 else 7),
         )
 
     bounds, sums = {}, {}
@@ -321,9 +338,6 @@
             value = value + decode(sin[e, d, r], bound_in[e, 1 if d == 0 else 7])
         return value
 
-    def w_copy(r):
-        return remote(zout.at[r], zin.at[r], w_s.at[r], w_r.at[r], line(r))
-
     def pass_on(steps, d, r):
         dist = begins(d, r) - steps
         limit = mine + near_sum(d, steps)
@@ -331,35 +345,33 @@
         yout[d, dist - 1, r] = encode(value, limit)
         start(y_copy(d, dist, r))
 
-    def reduced(r):
-        value = own(y, r)
+    for d, r in order:
+        pass_on(1, d, r)
+    for d in range(2):
+        for k in range(2):
+            limit_out[d, k] = mine + near_sum(d, k + 2)
+    for r in range(1, 4):
         for d in range(2):
-            value = value + arrived(d, 0, r)
-        return value
-
-    def send_reduced(r):
-        zout[r] = encode(reduced(r), total_out[...])
-        start(w_copy(r))
-
-    for steps, d, r in ((1, 0, 1), (1, 1, 2), (1, 0, 3), (1, 1, 1), (2, 0, 1), (2, 1, 2), (1, 0, 2), (1, 1, 3)):
-        pass_on(steps, d, r)
-    total_out[...] = mine + near_sum(0, 4) + near_sum(1, 3)
+            start(t_copy(d, r))
+    for steps in (2, 3):
+        for d, r in order:
+            if begins(d, r) > steps:
+                pass_on(steps, d, r)
+
+    result = own(y, 0)
     for r in range(1, 4):
-        start(t_copy(r))
-    for steps, d, r in ((2, 0, 3), (2, 1, 1), (3, 0, 1), (1, 1, 0), (2, 0, 2), (3, 1, 2), (1, 0, 0), (2, 1, 3), (3, 0, 3)):
-        pass_on(steps, d, r)
-    send_reduced(1)
-    pass_on(2, 1, 0)
-    send_reduced(2)
-    pass_on(2, 0, 0)
-    send_reduced(3)
-    pass_on(3, 1, 0)
-    result = reduced(0)
-    settle(len(started) - 10)
-    for r in range(1, 4):
-        t_copy(r).wait_recv()
-        w_copy(r).wait_recv()
-        result = result + decode(zin[r], total_in[r])
+        v_copy(r).wait_recv()
+        for e in range(2):
+            w_copy(e, r).wait_recv()
+            result = result + decode(zin[e, r], line_bound[r, e])
+    settle(len(started) - 12)
+    for d, r in order[4:] + order[:4]:
+        if r == 0:
+            result = result + arrived(d, 0, 0)
+        else:
+            t_copy(d, r).wait_recv()
+            y_copy(d, 1, r).wait_recv()
+            result = result + decode(yin[d, 0, r], limit_in[d, r])
     out[...] = result
     settle(len(started))
 
@@ -386,14 +398,15 @@
             vmem((2, 8, 256), F32),
             vmem((2, 8, 256), F32),
             vmem((2, 8, 8, 256), F32),
-            vmem((8, 256), F32),
-            vmem((4, 8, 256), F32),
+            vmem((4, 2, 8, 256), F32),
+            vmem((2, 2, 8, 256), F32),
+            vmem((2, 4, 8, 256), F32),
             vmem((2, 2, 4, ROWS, 256), jnp.bfloat16),
             vmem((2, 2, 4, ROWS, 256), jnp.bfloat16),
             vmem((2, 3, 4, ROWS, 256), jnp.bfloat16),
             vmem((2, 3, 4, ROWS, 256), jnp.bfloat16),
-            vmem((4, ROWS, 256), jnp.bfloat16),
-            vmem((4, ROWS, 256), jnp.bfloat16),
+            vmem((2, 4, ROWS, 256), jnp.bfloat16),
+            vmem((2, 4, ROWS, 256), jnp.bfloat16),
             dma((2, 2)),
             dma,
             dma((2, 2, 2, 2)), dma((2, 2, 2, 2)),
@@ -403,9 +416,10 @@
             dma((2, 16)), dma((2, 16)),
             dma((2, 8)), dma((2, 8)),
             dma((4,)), dma((4,)),
+            dma((2, 4)), dma((2, 4)),
             dma((2, 2, 4)), dma((2, 2, 4)),
             dma((2, 3, 4)), dma((2, 3, 4)),
-            dma((4,)), dma((4,)),
+            dma((2, 4)), dma((2, 4)),
         ],
         compiler_params=pltpu.CompilerParams(
             collective_id=0, has_side_effects=True, vmem_limit_bytes=56 * 2**20

time: 120 us -> 119 us (level)
    pallas_call x1, Pallas kernels: 116 us -> 115 us  [body(): pl.pallas_call(kernel, out_shape=jax.ShapeDtypeStruct((ROWS, 256), F32),...]
where the time goes in v4:
time: 119 us; the launch traced here: 117 us
  Pallas kernels  115 us (97%)
  local copies, waits for them, and re-layouts  1.55 us (1%)
    pallas_call x1, Pallas kernels, body(): pl.pallas_call(kernel, out_shape=jax.ShapeDtypeStruct((ROWS, 256), F32),...  115 us

profile of v4, /device:TPU:6, one launch (start us, length us, event | category | flops | bytes accessed | tf_op | source)
XLA Modules:
  0.0 117.1 jit_solution(14333666896836048373)
XLA Ops:
  0.7 114.9 %shard_map.37 = f32[112,256]{1,0:T(8,128)} custom-call(bf16[2,64,3584]{2,1,0:T(8,128)(2,1)} %act.1, bf16[2,1024,256]{2,1,0:T(8,128)(2,1)} %grads_in.1, f32[1]{0:T(128)S(6)} %copy.5.clip), custom_call_target="tpu_custom_call" | custom-call | flops 3758096384 | bytes 20000000 | tf_op jit(solution)/shard_map/pallas_call | solution.py:381
  115.5 1.6 %copy.6 = f32[112,256]{1,0:T(8,128)} copy(f32[112,256]{1,0:T(8,128)} %shard_map.37) | data formatting | bytes 229376

commit v5 on v4

--- a/solution.py
+++ b/solution.py
@@ -10,7 +10,7 @@
 MESH = pl.DeviceIdType.MESH
 F32 = jnp.float32
 NX, NY, NZL, NZH = 4, 8, 4, 2
-HALF = 32
+HALF, PIECE = 32, 16
 ROWS = 112
 TILE = 512
 POWER, SHIFT = 11, 120
@@ -77,27 +77,32 @@
         copy.start()
         started.append(copy)
 
-    def x_copy(e, far, d, h):
+    def piece(block, t):
+        return block if t is None else block.at[pl.ds(PIECE * t, PIECE)]
+
+    def x_copy(e, far, d, h, t=None):
         return remote(
-            unit(e, far, OWN, 0, h), unit(e, far, FROM_LEFT if d == 0 else FROM_RIGHT, 0, h),
-            x_s.at[e, far, d, h], x_r.at[e, far, d, h], x_next[d],
-        )
-
-    def f_copy(e, far, d):
+            piece(unit(e, far, OWN, 0, h), t),
+            piece(unit(e, far, FROM_LEFT if d == 0 else FROM_RIGHT, 0, h), t),
+            x_s.at[e, far, d, h, t or 0], x_r.at[e, far, d, h, t or 0], x_next[d],
+        )
+
+    def f_copy(e, far, d, t=None):
         return remote(
-            unit(e, far, FROM_LEFT if d == 0 else FROM_RIGHT, 0, d), unit(e, far, FAR, 0, d),
-            f_s.at[e, far, d], f_r.at[e, far, d], x_next[d],
-        )
-
-    def z_copy(e, d, leg):
-        src = unit(e, 0, OWN, 0, d) if leg == 0 else relay.at[e, d]
-        dst = relay.at[e, d] if leg == 0 else unit(e, 1, OWN, 0, d)
-        return remote(src, dst, z_s.at[e, d, leg], z_r.at[e, d, leg], z_far[d])
-
-    def d_copy(e, far, pos, h):
+            piece(unit(e, far, FROM_LEFT if d == 0 else FROM_RIGHT, 0, d), t),
+            piece(unit(e, far, FAR, 0, d), t),
+            f_s.at[e, far, d, t or 0], f_r.at[e, far, d, t or 0], x_next[d],
+        )
+
+    def z_copy(e, d, leg, t):
+        src = piece(unit(e, 0, OWN, 0, d), t) if leg == 0 else relay.at[e, d, t]
+        dst = relay.at[e, d, t] if leg == 0 else piece(unit(e, 1, OWN, 0, d), t)
+        return remote(src, dst, z_s.at[e, d, leg, t], z_r.at[e, d, leg, t], z_far[d])
+
+    def d_copy(e, far, pos, h, t=None):
         return remote(
-            unit(e, far, pos, 0, h), unit(e, far, pos, 1, h),
-            d_s.at[e, far, pos, h], d_r.at[e, far, pos, h], other,
+            piece(unit(e, far, pos, 0, h), t), piece(unit(e, far, pos, 1, h), t),
+            d_s.at[e, far, pos, h, t or 0], d_r.at[e, far, pos, h, t or 0], other,
         )
 
     loads = {
@@ -110,6 +115,10 @@
         load.start()
     grads_load = pltpu.make_async_copy(grads_in, grads, grads_sem)
     grads_load.start()
+
+    def send_z(e, t):
+        for d in range(2):
+            start(z_copy(e, d, 0, t))
 
     barrier = pltpu.get_barrier_semaphore()
     greeted = [to for _, to in tp_peers] + list(z_far.values())
@@ -123,8 +132,7 @@
         for h in range(2):
             loads[e, h].wait()
         if e == 0:
-            start(z_copy(0, 0, 0))
-            start(z_copy(0, 1, 0))
+            send_z(0, 0)
         for h in range(2):
             for d in range(2):
                 start(x_copy(e, 0, d, h if d == 0 else 1 - h))
@@ -142,36 +150,37 @@
                     rows = pl.ds(pl.multiple_of(block * 64, 64), 64)
                     gr[e, 8 * far + 2 * pos + core] = grads[e, rows, :]
 
-    def pass_relay(e):
+    def pass_relay(e, t):
         for d in range(2):
-            z_copy(e, d, 0).wait_recv()
-            start(z_copy(e, d, 1))
-
-    def take_z(e):
+            z_copy(e, d, 0, t).wait_recv()
+            start(z_copy(e, d, 1, t))
+
+    def take_z(e, t):
         for d in range(2):
-            z_copy(e, d, 1).wait_recv()
+            z_copy(e, d, 1, t).wait_recv()
             for k in range(2):
-                start(x_copy(e, 1, k, d))
-            start(d_copy(e, 1, OWN, d))
-
-    def take_x(e, far):
+                start(x_copy(e, 1, k, d, t))
+            start(d_copy(e, 1, OWN, d, t))
+
+    def take_x(e, far, t=None):
         for step in range(2):
             for d in range(2):
                 h = d if step == 0 else 1 - d
-                x_copy(e, far, d, h).wait_recv()
+                x_copy(e, far, d, h, t).wait_recv()
                 if step == 0:
-                    start(f_copy(e, far, d))
-                start(d_copy(e, far, FROM_LEFT if d == 0 else FROM_RIGHT, h))
-
-    def take_far(e, far):
+                    start(f_copy(e, far, d, t))
+                start(d_copy(e, far, FROM_LEFT if d == 0 else FROM_RIGHT, h, t))
+
+    def take_far(e, far, t=None):
         for d in range(2):
-            f_copy(e, far, d).wait_recv()
-            start(d_copy(e, far, FAR, d))
+            f_copy(e, far, d, t).wait_recv()
+            start(d_copy(e, far, FAR, d, t))
 
     def wait_core(e, far, positions):
         for pos in positions:
             for h in range(2):
-                d_copy(e, far, pos, h).wait_recv()
+                for t in (0, 1) if far else (None,):
+                    d_copy(e, far, pos, h, t).wait_recv()
 
     def multiply(e, lo, hi):
         first, last = lo == 0, hi == 8
@@ -246,38 +255,47 @@
         for k in (1, 7, 2, 6, 3, 5, 4):
             start(b_copy(e, k))
 
-    pass_relay(0)
+    pass_relay(0, 0)
+    send_z(0, 1)
     take_x(0, 0)
     take_x(1, 0)
-    take_z(0)
-    start(z_copy(1, 0, 0))
-    start(z_copy(1, 1, 0))
+    pass_relay(0, 1)
+    take_z(0, 0)
+    send_z(1, 0)
     wait_core(0, 0, [OWN, FROM_RIGHT, FROM_LEFT])
     multiply(0, 0, 3)
-    pass_relay(1)
+    pass_relay(1, 0)
+    take_z(0, 1)
+    send_z(1, 1)
     wait_core(1, 0, [OWN, FROM_RIGHT, FROM_LEFT])
     multiply(1, 0, 3)
     take_far(0, 0)
     take_far(1, 0)
-    take_x(0, 1)
-    take_z(1)
+    take_x(0, 1, 0)
+    pass_relay(1, 1)
+    take_z(1, 0)
+    take_x(0, 1, 1)
     wait_core(0, 0, [FAR])
     wait_core(0, 1, [OWN, FROM_RIGHT, FROM_LEFT])
     multiply(0, 3, 7)
-    take_far(0, 1)
+    take_z(1, 1)
+    take_far(0, 1, 0)
+    take_far(0, 1, 1)
     wait_core(0, 1, [FAR])
     multiply(0, 7, 8)
+    take_x(1, 1, 0)
     wait_core(1, 0, [FAR])
     wait_core(1, 1, [OWN])
     multiply(1, 3, 5)
-    take_x(1, 1)
+    take_x(1, 1, 1)
     most0 = first_hop(0)
     wait_core(1, 1, [FROM_RIGHT, FROM_LEFT])
     multiply(1, 5, 7)
     factor0 = factor(0)
     bound0 = factor0 * most0
     send_bound(0, bound0)
-    take_far(1, 1)
+    take_far(1, 1, 0)
+    take_far(1, 1, 1)
     wait_core(1, 1, [FAR])
     multiply(1, 7, 8)
     most1 = first_hop(1)
@@ -390,7 +408,7 @@
         scratch_shapes=[
             vmem((2, 1024, 256), jnp.bfloat16),
             vmem((2, 32, HALF, 3584), jnp.bfloat16),
-            vmem((2, 2, HALF, 3584), jnp.bfloat16),
+            vmem((2, 2, 2, PIECE, 3584), jnp.bfloat16),
             vmem((2, 16, 64, 256), jnp.bfloat16),
             vmem((2, 3584, 256), F32),
             vmem((2, 8, 256), F32),
@@ -409,10 +427,10 @@
             vmem((2, 4, ROWS, 256), jnp.bfloat16),
             dma((2, 2)),
             dma,
+            dma((2, 2, 2, 2, 2)), dma((2, 2, 2, 2, 2)),
             dma((2, 2, 2, 2)), dma((2, 2, 2, 2)),
-            dma((2, 2, 2)), dma((2, 2, 2)),
-            dma((2, 2, 2)), dma((2, 2, 2)),
-            dma((2, 2, 4, 2)), dma((2, 2, 4, 2)),
+            dma((2, 2, 2, 2)), dma((2, 2, 2, 2)),
+            dma((2, 2, 4, 2, 2)), dma((2, 2, 4, 2, 2)),
             dma((2, 16)), dma((2, 16)),
             dma((2, 8)), dma((2, 8)),
             dma((4,)), dma((4,)),

time: 119 us -> 122 us (1.025)
  Pallas kernels: 115 us -> 118 us
    pallas_call x1, Pallas kernels: 115 us -> 118 us  [body(): pl.pallas_call(kernel, out_shape=jax.ShapeDtypeStruct((ROWS, 256), F32),...]
where the time goes in v5:
time: 122 us; the launch traced here: 121 us
  Pallas kernels  118 us (97%)
  local copies, waits for them, and re-layouts  1.55 us (1%)
    pallas_call x1, Pallas kernels, body(): pl.pallas_call(kernel, out_shape=jax.ShapeDtypeStruct((ROWS, 256), F32),...  118 us

profile of v5, /device:TPU:6, one launch (start us, length us, event | category | flops | bytes accessed | tf_op | source)
XLA Modules:
  0.0 120.6 jit_solution(6467511923366457292)
XLA Ops:
  0.7 118.4 %shard_map.37 = f32[112,256]{1,0:T(8,128)} custom-call(bf16[2,64,3584]{2,1,0:T(8,128)(2,1)} %act.1, bf16[2,1024,256]{2,1,0:T(8,128)(2,1)} %grads_in.1, f32[1]{0:T(128)S(6)} %copy.5.clip), custom_call_target="tpu_custom_call" | custom-call | flops 3758096384 | bytes 20000000 | tf_op jit(solution)/shard_map/pallas_call | solution.py:399
  119.0 1.6 %copy.6 = f32[112,256]{1,0:T(8,128)} copy(f32[112,256]{1,0:T(8,128)} %shard_map.37) | data formatting | bytes 229376

commit v6 on v4

--- a/solution.py
+++ b/solution.py
@@ -52,7 +52,8 @@
     def line(r, dy=0):
         return (lax.rem(y + dy, 8) * 4 + lax.rem(zl + r, 4), tp)
 
-    tp_peers = [(i, peer(dx=(i // 2) % 4, dz=4 * (i // 8), dc=i % 2)) for i in range(15, 0, -1)]
+    square = [peer(dc=1), peer(dz=4), peer(dc=1, dz=4)]
+    row = [peer(dx=k) for k in range(1, 4)]
     z_far = {0: peer(dz=2), 1: peer(dz=6)}
     x_next = {0: peer(dx=1), 1: peer(dx=3)}
     y_next = {0: peer(dy=1), 1: peer(dy=7)}
@@ -112,7 +113,7 @@
     grads_load.start()
 
     barrier = pltpu.get_barrier_semaphore()
-    greeted = [to for _, to in tp_peers] + list(z_far.values())
+    greeted = square + row + list(z_far.values())
     greeted += [peer(dy=k) for k in range(1, 8)]
     greeted += [line(r, dy) for r in range(1, 4) for dy in (0, 1, 7)]
     for to in greeted:
@@ -172,6 +173,12 @@
         for pos in positions:
             for h in range(2):
                 d_copy(e, far, pos, h).wait_recv()
+
+    def norm_copies(e, stage):
+        return [
+            remote(sq.at[e, stage], sq_in.at[e, stage, i], n_s.at[e, stage, i], n_r.at[e, stage, i], to)
+            for i, to in enumerate((square, row)[stage])
+        ]
 
     def multiply(e, lo, hi):
         first, last = lo == 0, hi == 8
@@ -194,10 +201,10 @@
         none = jnp.zeros((8, 256), F32)
         total, most = lax.fori_loop(0, 3584 // TILE, body, (none, none))
         if last:
-            sq[e] = total
-            top[e] = most
-            for i, to in tp_peers:
-                start(remote(sq.at[e], sq_in.at[e, i], n_s.at[e, i], n_r.at[e, i], to))
+            sq[e, 0] = total
+            for copy in norm_copies(e, 0):
+                start(copy)
+            top[e] = jnp.broadcast_to(jnp.max(most, axis=(0, 1), keepdims=True), (8, 256)) * 1.0001 + 1e-35
 
     def begins(d, r):
         return 4 if (r in (1, 3)) == (d == 0) else 3
@@ -209,9 +216,6 @@
     def ahead(d, dist):
         return lax.rem(y + (dist if d == 0 else 8 - dist), 8)
 
-    def tile_max(value):
-        return jnp.broadcast_to(jnp.max(value, axis=(0, 1), keepdims=True), (8, 256))
-
     order = [(0, 1), (1, 2), (0, 3), (1, 0), (1, 1), (0, 2), (1, 3), (0, 0)]
 
     def s_copy(e, d, r):
@@ -220,31 +224,37 @@
     def w_copy(e, r):
         return remote(zout.at[e, r], zin.at[e, r], w_s.at[e, r], w_r.at[e, r], line(r))
 
-    def first_hop(e):
-        most = tile_max(top[e]) * 1.0001 + 1e-35
-        for d, r in order:
-            sout[e, d, r] = encode(block(e, ahead(d, begins(d, r)), r), most)
+    def first_hop(e, chains):
+        limit = top[e]
+        for d, r in chains:
+            sout[e, d, r] = encode(block(e, ahead(d, begins(d, r)), r), limit)
             start(s_copy(e, d, r))
+
+    def send_raw(e):
+        limit = top[e]
         for r in range(1, 4):
-            zout[e, r] = encode(block(e, y, r), most)
+            zout[e, r] = encode(block(e, y, r), limit)
             start(w_copy(e, r))
-        return most
+
+    def gathered(e, stage):
+        total = sq[e, stage]
+        for i, copy in enumerate(norm_copies(e, stage)):
+            copy.wait_recv()
+            total = total + sq_in[e, stage, i]
+        return total
+
+    def pass_norm(e):
+        sq[e, 1] = gathered(e, 0)
+        for copy in norm_copies(e, 1):
+            start(copy)
 
     def factor(e):
-        total = sq[e]
-        for i, to in tp_peers:
-            remote(sq.at[e], sq_in.at[e, i], n_s.at[e, i], n_r.at[e, i], to).wait_recv()
-            total = total + sq_in[e, i]
+        total = gathered(e, 1)
         norm = jnp.sqrt(jnp.broadcast_to(jnp.sum(total, axis=(0, 1), keepdims=True), (8, 256)))
         return jnp.minimum(1.0, clip[0] / (norm + 1e-06))
 
-    def b_copy(e, k):
-        return remote(bound.at[e], bound_in.at[e, k], b_s.at[e, k], b_r.at[e, k], peer(dy=k))
-
-    def send_bound(e, value):
-        bound[e] = value
-        for k in (1, 7, 2, 6, 3, 5, 4):
-            start(b_copy(e, k))
+    def b_copy(k):
+        return remote(bound, bound_in.at[k], b_s.at[k], b_r.at[k], peer(dy=k))
 
     pass_relay(0)
     take_x(0, 0)
@@ -271,20 +281,26 @@
     wait_core(1, 1, [OWN])
     multiply(1, 3, 5)
     take_x(1, 1)
-    most0 = first_hop(0)
+    first_hop(0, order[:4])
+    pass_norm(0)
+    first_hop(0, order[4:])
+    send_raw(0)
     wait_core(1, 1, [FROM_RIGHT, FROM_LEFT])
     multiply(1, 5, 7)
-    factor0 = factor(0)
-    bound0 = factor0 * most0
-    send_bound(0, bound0)
     take_far(1, 1)
     wait_core(1, 1, [FAR])
     multiply(1, 7, 8)
-    most1 = first_hop(1)
+    first_hop(1, order[:4])
+    pass_norm(1)
+    first_hop(1, order[4:])
+    factor0 = factor(0)
     factor1 = factor(1)
-    bound1 = factor1 * most1
-    send_bound(1, bound1)
-    mine = bound0 + bound1
+    bound[0] = factor0 * top[0]
+    bound[1] = factor1 * top[1]
+    for k in (1, 7, 2, 6, 3, 5, 4):
+        start(b_copy(k))
+    mine = bound[0] + bound[1]
+    send_raw(1)
 
     def own(row_y, r):
         terms = [
@@ -296,9 +312,6 @@
     def v_copy(r):
         return remote(bound, line_bound.at[r], v_s.at[r], v_r.at[r], line(r))
 
-    for r in range(1, 4):
-        start(v_copy(r))
-
     def t_copy(d, r):
         return remote(
             limit_out.at[d, begins(d, r) - 3], limit_in.at[d, r], t_s.at[d, r], t_r.at[d, r],
@@ -316,9 +329,8 @@
 
     def near(k):
         if k not in bounds:
-            for e in range(2):
-                b_copy(e, k).wait_recv()
-            bounds[k] = bound_in[0, k] + bound_in[1, k]
+            b_copy(k).wait_recv()
+            bounds[k] = bound_in[k, 0] + bound_in[k, 1]
         return bounds[k]
 
     def near_sum(d, n):
@@ -335,7 +347,7 @@
         value = 0.0
         for e in range(2):
             s_copy(e, d, r).wait_recv()
-            value = value + decode(sin[e, d, r], bound_in[e, 1 if d == 0 else 7])
+            value = value + decode(sin[e, d, r], bound_in[1 if d == 0 else 7, e])
         return value
 
     def pass_on(steps, d, r):
@@ -347,16 +359,19 @@
 
     for d, r in order:
         pass_on(1, d, r)
+    for d, r in order:
+        if begins(d, r) > 2:
+            pass_on(2, d, r)
     for d in range(2):
         for k in range(2):
             limit_out[d, k] = mine + near_sum(d, k + 2)
     for r in range(1, 4):
+        start(v_copy(r))
         for d in range(2):
             start(t_copy(d, r))
-    for steps in (2, 3):
-        for d, r in order:
-            if begins(d, r) > steps:
-                pass_on(steps, d, r)
+    for d, r in order:
+        if begins(d, r) > 3:
+            pass_on(3, d, r)
 
     result = own(y, 0)
     for r in range(1, 4):
@@ -393,11 +408,11 @@
             vmem((2, 2, HALF, 3584), jnp.bfloat16),
             vmem((2, 16, 64, 256), jnp.bfloat16),
             vmem((2, 3584, 256), F32),
-            vmem((2, 8, 256), F32),
-            vmem((2, 16, 8, 256), F32),
+            vmem((2, 2, 8, 256), F32),
+            vmem((2, 2, 3, 8, 256), F32),
             vmem((2, 8, 256), F32),
             vmem((2, 8, 256), F32),
-            vmem((2, 8, 8, 256), F32),
+            vmem((8, 2, 8, 256), F32),
             vmem((4, 2, 8, 256), F32),
             vmem((2, 2, 8, 256), F32),
             vmem((2, 4, 8, 256), F32),
@@ -413,8 +428,8 @@
             dma((2, 2, 2)), dma((2, 2, 2)),
             dma((2, 2, 2)), dma((2, 2, 2)),
             dma((2, 2, 4, 2)), dma((2, 2, 4, 2)),
-            dma((2, 16)), dma((2, 16)),
-            dma((2, 8)), dma((2, 8)),
+            dma((2, 2, 3)), dma((2, 2, 3)),
+            dma((8,)), dma((8,)),
             dma((4,)), dma((4,)),
             dma((2, 4)), dma((2, 4)),
             dma((2, 2, 4)), dma((2, 2, 4)),

time: 119 us -> 120 us (level); the launches traced: 117 us -> 120 us
  Pallas kernels: 115 us -> 118 us
    pallas_call x1, Pallas kernels: 115 us -> 118 us  [body(): pl.pallas_call(kernel, out_shape=jax.ShapeDtypeStruct((ROWS, 256), F32),...]
where the time goes in v6:
time: 120 us
  Pallas kernels  118 us (98%)
  local copies, waits for them, and re-layouts  1.55 us (1%)
    pallas_call x1, Pallas kernels, body(): pl.pallas_call(kernel, out_shape=jax.ShapeDtypeStruct((ROWS, 256), F32),...  118 us

profile of v6, /device:TPU:6, one launch (start us, length us, event | category | flops | bytes accessed | tf_op | source)
XLA Modules:
  0.0 120.3 jit_solution(5898605102889986992)
XLA Ops:
  0.7 118.1 %shard_map.37 = f32[112,256]{1,0:T(8,128)} custom-call(bf16[2,64,3584]{2,1,0:T(8,128)(2,1)} %act.1, bf16[2,1024,256]{2,1,0:T(8,128)(2,1)} %grads_in.1, f32[1]{0:T(128)S(6)} %copy.5.clip), custom_call_target="tpu_custom_call" | custom-call | flops 3758096384 | bytes 20000000 | tf_op jit(solution)/shard_map/pallas_call | solution.py:396
  118.8 1.6 %copy.6 = f32[112,256]{1,0:T(8,128)} copy(f32[112,256]{1,0:T(8,128)} %shard_map.37) | data formatting | bytes 229376

commit v7 on v4

--- a/solution.py
+++ b/solution.py
@@ -77,10 +77,13 @@
         copy.start()
         started.append(copy)
 
-    def x_copy(e, far, d, h):
+    def whole(e, far, pos, core):
+        return buf.at[e, pl.ds(16 * far + 4 * pos + 2 * core, 2)]
+
+    def x_copy(e, far, d):
         return remote(
-            unit(e, far, OWN, 0, h), unit(e, far, FROM_LEFT if d == 0 else FROM_RIGHT, 0, h),
-            x_s.at[e, far, d, h], x_r.at[e, far, d, h], x_next[d],
+            whole(e, far, OWN, 0), whole(e, far, FROM_LEFT if d == 0 else FROM_RIGHT, 0),
+            x_s.at[e, far, d], x_r.at[e, far, d], x_next[d],
         )
 
     def f_copy(e, far, d):
@@ -94,10 +97,9 @@
         dst = relay.at[e, d] if leg == 0 else unit(e, 1, OWN, 0, d)
         return remote(src, dst, z_s.at[e, d, leg], z_r.at[e, d, leg], z_far[d])
 
-    def d_copy(e, far, pos, h):
+    def d_copy(e, far, pos):
         return remote(
-            unit(e, far, pos, 0, h), unit(e, far, pos, 1, h),
-            d_s.at[e, far, pos, h], d_r.at[e, far, pos, h], other,
+            whole(e, far, pos, 0), whole(e, far, pos, 1), d_s.at[e, far, pos], d_r.at[e, far, pos], other
         )
 
     loads = {
@@ -125,11 +127,9 @@
         if e == 0:
             start(z_copy(0, 0, 0))
             start(z_copy(0, 1, 0))
-        for h in range(2):
-            for d in range(2):
-                start(x_copy(e, 0, d, h if d == 0 else 1 - h))
-        for h in range(2):
-            start(d_copy(e, 0, OWN, h))
+        for d in range(2):
+            start(x_copy(e, 0, d))
+        start(d_copy(e, 0, OWN))
 
     grads_load.wait()
     for e in range(2):
@@ -150,28 +150,24 @@
     def take_z(e):
         for d in range(2):
             z_copy(e, d, 1).wait_recv()
-            for k in range(2):
-                start(x_copy(e, 1, k, d))
-            start(d_copy(e, 1, OWN, d))
+        for d in range(2):
+            start(x_copy(e, 1, d))
+        start(d_copy(e, 1, OWN))
 
     def take_x(e, far):
-        for step in range(2):
-            for d in range(2):
-                h = d if step == 0 else 1 - d
-                x_copy(e, far, d, h).wait_recv()
-                if step == 0:
-                    start(f_copy(e, far, d))
-                start(d_copy(e, far, FROM_LEFT if d == 0 else FROM_RIGHT, h))
+        for d in range(2):
+            x_copy(e, far, d).wait_recv()
+            start(f_copy(e, far, d))
+            start(d_copy(e, far, FROM_LEFT if d == 0 else FROM_RIGHT))
 
     def take_far(e, far):
         for d in range(2):
             f_copy(e, far, d).wait_recv()
-            start(d_copy(e, far, FAR, d))
+        start(d_copy(e, far, FAR))
 
     def wait_core(e, far, positions):
         for pos in positions:
-            for h in range(2):
-                d_copy(e, far, pos, h).wait_recv()
+            d_copy(e, far, pos).wait_recv()
 
     def multiply(e, lo, hi):
         first, last = lo == 0, hi == 8
@@ -409,10 +405,10 @@
             vmem((2, 4, ROWS, 256), jnp.bfloat16),
             dma((2, 2)),
             dma,
-            dma((2, 2, 2, 2)), dma((2, 2, 2, 2)),
             dma((2, 2, 2)), dma((2, 2, 2)),
             dma((2, 2, 2)), dma((2, 2, 2)),
-            dma((2, 2, 4, 2)), dma((2, 2, 4, 2)),
+            dma((2, 2, 2)), dma((2, 2, 2)),
+            dma((2, 2, 4)), dma((2, 2, 4)),
             dma((2, 16)), dma((2, 16)),
             dma((2, 8)), dma((2, 8)),
             dma((4,)), dma((4,)),

time: 119 us -> 119 us (level)
  no operation moved by 1% of the time
where the time goes in v7:
time: 119 us; the launch traced here: 117 us
  Pallas kernels  115 us (97%)
  local copies, waits for them, and re-layouts  1.55 us (1%)
    pallas_call x1, Pallas kernels, body(): pl.pallas_call(kernel, out_shape=jax.ShapeDtypeStruct((ROWS, 256), F32),...  115 us

profile of v7, /device:TPU:6, one launch (start us, length us, event | category | flops | bytes accessed | tf_op | source)
XLA Modules:
  0.0 117.5 jit_solution(8649931214297492869)
XLA Ops:
  0.7 115.3 %shard_map.37 = f32[112,256]{1,0:T(8,128)} custom-call(bf16[2,64,3584]{2,1,0:T(8,128)(2,1)} %act.1, bf16[2,1024,256]{2,1,0:T(8,128)(2,1)} %grads_in.1, f32[1]{0:T(128)S(6)} %copy.5.clip), custom_call_target="tpu_custom_call" | custom-call | flops 3758096384 | bytes 20000000 | tf_op jit(solution)/shard_map/pallas_call | solution.py:377
  115.9 1.6 %copy.6 = f32[112,256]{1,0:T(8,128)} copy(f32[112,256]{1,0:T(8,128)} %shard_map.37) | data formatting | bytes 229376

commit v8 on v4

--- a/solution.py
+++ b/solution.py
@@ -252,11 +252,10 @@
     take_z(0)
     start(z_copy(1, 0, 0))
     start(z_copy(1, 1, 0))
-    wait_core(0, 0, [OWN, FROM_RIGHT, FROM_LEFT])
-    multiply(0, 0, 3)
+    for e in range(2):
+        wait_core(e, 0, [OWN, FROM_RIGHT, FROM_LEFT])
+        multiply(e, 0, 3)
     pass_relay(1)
-    wait_core(1, 0, [OWN, FROM_RIGHT, FROM_LEFT])
-    multiply(1, 0, 3)
     take_far(0, 0)
     take_far(1, 0)
     take_x(0, 1)
@@ -267,13 +266,11 @@
     take_far(0, 1)
     wait_core(0, 1, [FAR])
     multiply(0, 7, 8)
-    wait_core(1, 0, [FAR])
-    wait_core(1, 1, [OWN])
-    multiply(1, 3, 5)
     take_x(1, 1)
     most0 = first_hop(0)
-    wait_core(1, 1, [FROM_RIGHT, FROM_LEFT])
-    multiply(1, 5, 7)
+    wait_core(1, 0, [FAR])
+    wait_core(1, 1, [OWN, FROM_RIGHT, FROM_LEFT])
+    multiply(1, 3, 7)
     factor0 = factor(0)
     bound0 = factor0 * most0
     send_bound(0, bound0)

time: 119 us -> 118 us (level)
  no operation moved by 1% of the time
where the time goes in v8:
time: 118 us; the launch traced here: 117 us
  Pallas kernels  115 us (97%)
  local copies, waits for them, and re-layouts  1.55 us (1%)
    pallas_call x1, Pallas kernels, body(): pl.pallas_call(kernel, out_shape=jax.ShapeDtypeStruct((ROWS, 256), F32),...  115 us

profile of v8, /device:TPU:6, one launch (start us, length us, event | category | flops | bytes accessed | tf_op | source)
XLA Modules:
  0.0 117.3 jit_solution(8017936526119823949)
XLA Ops:
  0.7 115.0 %shard_map.37 = f32[112,256]{1,0:T(8,128)} custom-call(bf16[2,64,3584]{2,1,0:T(8,128)(2,1)} %act.1, bf16[2,1024,256]{2,1,0:T(8,128)(2,1)} %grads_in.1, f32[1]{0:T(128)S(6)} %copy.5.clip), custom_call_target="tpu_custom_call" | custom-call | flops 3758096384 | bytes 20000000 | tf_op jit(solution)/shard_map/pallas_call | solution.py:378
  115.7 1.6 %copy.6 = f32[112,256]{1,0:T(8,128)} copy(f32[112,256]{1,0:T(8,128)} %shard_map.37) | data formatting | bytes 229376
